TPU v7x, 256 devices: a whole 4x4x8 slice. The times are simulated.
256 devices in a mesh: row: 8 (over x, core), col: 32 (over y, z).
Axes of the slice: x: 4, y: 4, z: 8, core: 2. Of those that a mesh axis runs over, the one named last changes fastest.
Arguments:
- features: bfloat16 [65536, 256], P(('row', 'col')), may hold values from -6 to 6
- neighbours: int32 [10, 65536], P(None, ('row', 'col')), may hold values from 0 to 511, as said below
- halo_ids: int32 [256, 1, 256], P(('row', 'col')), may hold values from 0 to 255
- w_self: bfloat16 [256, 256], replicated, may hold values from -0.375 to 0.375
- w_neigh: bfloat16 [256, 256], replicated, may hold values from -0.75 to 0.75
- b_sage: float32 [256], replicated, may hold values from -3 to 3
- w_first: bfloat16 [512, 256], replicated, may hold values from -0.25 to 0.25
- b_first: float32 [256], replicated, may hold values from -3 to 3
- w_second: bfloat16 [256], replicated, may hold values from -1.5 to 1.5
- b_second: float32 [1], replicated, may hold values from -3 to 3
- src_owner: int32 [8, 32, 8192, 1], P('row', 'col'), may hold values from 0 to 31; in each aligned block of 8192 rows (0 to 8191, 8192 to 16383, ..., all dimensions but the last counted through in order) at most 320 rows name the same one
- src_local: int32 [8, 32, 8192], P('row', 'col'), may hold values from 0 to 255
- dst_index: int32 [8, 32, 8192], P('row', 'col'), may hold values from 0 to 2047
- labels: int32 [8, 32, 8192], P('row', 'col'), may hold values 0 or 1
Outputs:
- embeds: bfloat16 [65536, 256], P(('row', 'col'))
- logits: float32 [8, 32, 8192], P('row', 'col')
- node_grad: float32 [65536, 256], P(('row', 'col'))
- grad_self: float32 [256, 256], replicated
- grad_neigh: float32 [256, 256], replicated
- grad_bsage: float32 [256], replicated
- grad_first: float32 [32, 512, 256], P('col')
- grad_bfirst: float32 [32, 256], P('col')
- grad_second: float32 [32, 256], P('col')
Inputs may be any that keep to these rules, and one draw needn't show every extreme that they name: `neighbours`: in each partition every one of the 256 received rows (values 256 and up) is named by exactly one entry; the other entries name the partition's own rows. `src_owner`: among the 8192 edges of one tile at most 320 name the same source partition, and that many are reached.
All inputs are finite; a program needn't handle non-finite values. No bound on the sum of `labels` on one device may be relied on, other than what follows from the above.
Results may differ from a plain program's by a relative error of at most 0.0052.
Values may be sent and summed in bfloat16 or wider, within the bound.
No kernel may reach another device: no remote copies, remote signals or barrier semaphores. Data moves between devices by JAX's collectives and lax.ppermute only.
A program may use at most 128 MiB of HBM per device.

v0:
```python
import jax
import jax.numpy as jnp
from jax import lax
from jax.sharding import PartitionSpec as P


def per_device(
    features,
    neighbours,
    halo_ids,
    w_self,
    w_neigh,
    b_sage,
    w_first,
    b_first,
    w_second,
    b_second,
    src_owner,
    src_local,
    dst_index,
    labels,
):
    node_dev, feat_width = features.shape
    fanout = neighbours.shape[0]
    row_count = lax.axis_size("row")
    col_count = lax.axis_size("col")
    outgoing = features[halo_ids[0]]
    halo_count = outgoing.shape[0]
    outgoing = outgoing.reshape(halo_count, row_count, col_count, feat_width)
    received = lax.all_to_all(
        lax.all_to_all(outgoing, "row", split_axis=1, concat_axis=1, tiled=True),
        "col",
        split_axis=2,
        concat_axis=2,
        tiled=True,
    )
    extended = jnp.concatenate([features, received.reshape(-1, feat_width)], axis=0)
    gathered = extended[neighbours].astype(jnp.float32)
    aggregate = (jnp.sum(gathered, axis=0) / fanout).astype(jnp.bfloat16)
    embed_f = jnp.dot(features, w_self, preferred_element_type=jnp.float32)
    embed_f = embed_f + jnp.dot(aggregate, w_neigh, preferred_element_type=jnp.float32) + b_sage
    embeds = embed_f.astype(jnp.bfloat16)
    owners = src_owner[0, 0, :, 0]
    local_rows = src_local[0, 0]
    dest_rows = dst_index[0, 0]
    targets = labels[0, 0].astype(jnp.float32)
    edge_count = owners.shape[0]
    src_block = lax.all_gather(embeds, "col", axis=0, tiled=True)
    block_rows = owners * node_dev + local_rows
    src_embed = src_block[block_rows]
    dst_block = lax.all_gather(embeds, "row", axis=0, tiled=True)
    dst_embed = dst_block[dest_rows]
    w_src = w_first[:feat_width]
    w_dst = w_first[feat_width:]
    preact = jnp.dot(src_embed, w_src, preferred_element_type=jnp.float32)
    preact = preact + jnp.dot(dst_embed, w_dst, preferred_element_type=jnp.float32) + b_first
    gate_sig = jax.nn.sigmoid(preact)
    hidden = preact * gate_sig
    hidden_b = hidden.astype(jnp.bfloat16)
    logits = jnp.dot(hidden_b, w_second, preferred_element_type=jnp.float32) + b_second[0]
    dlogit = jax.nn.sigmoid(logits) - targets
    second_f = w_second.astype(jnp.float32)
    dpreact = dlogit[:, None] * second_f[None, :] * gate_sig * (1.0 + preact * (1.0 - gate_sig))
    dpreact_b = dpreact.astype(jnp.bfloat16)
    part_second = jnp.sum(hidden * dlogit[:, None], axis=0)
    part_bfirst = jnp.sum(dpreact, axis=0)
    grad_src = jnp.dot(src_embed.T, dpreact_b, preferred_element_type=jnp.float32)
    grad_dst = jnp.dot(dst_embed.T, dpreact_b, preferred_element_type=jnp.float32)
    part_first = jnp.concatenate([grad_src, grad_dst], axis=0)
    decoder_sums = lax.psum((part_first, part_bfirst, part_second), "row")
    src_rows_g = jnp.dot(dpreact_b, w_src.T, preferred_element_type=jnp.float32).astype(
        jnp.bfloat16
    )
    dst_rows_g = jnp.dot(dpreact_b, w_dst.T, preferred_element_type=jnp.float32).astype(
        jnp.bfloat16
    )
    src_acc = (
        jnp.zeros((src_block.shape[0], feat_width), jnp.float32)
        .at[block_rows]
        .add(src_rows_g.astype(jnp.float32))
    )
    src_grad = lax.psum_scatter(src_acc, "col", scatter_dimension=0, tiled=True)
    dest_acc = (
        jnp.zeros((dst_block.shape[0], feat_width), jnp.float32)
        .at[dest_rows]
        .add(dst_rows_g.astype(jnp.float32))
    )
    dest_grad = lax.psum_scatter(dest_acc, "row", scatter_dimension=0, tiled=True)
    node_grad = src_grad + dest_grad
    node_grad_b = node_grad.astype(jnp.bfloat16)
    part_self = jnp.dot(features.T, node_grad_b, preferred_element_type=jnp.float32)
    part_neigh = jnp.dot(aggregate.T, node_grad_b, preferred_element_type=jnp.float32)
    part_bsage = jnp.sum(node_grad, axis=0)
    encoder_sums = lax.psum((part_self, part_neigh, part_bsage), ("row", "col"))
    return (
        embeds,
        logits.reshape(1, 1, edge_count),
        node_grad,
        encoder_sums[0],
        encoder_sums[1],
        encoder_sums[2],
        decoder_sums[0][None],
        decoder_sums[1][None],
        decoder_sums[2][None],
    )


def solution(mesh):
    placed = (
        P(("row", "col"), None),
        P(None, ("row", "col")),
        P(("row", "col"), None, None),
        P(),
        P(),
        P(),
        P(),
        P(),
        P(),
        P(),
        P("row", "col", None, None),
        P("row", "col", None),
        P("row", "col", None),
        P("row", "col", None),
    )
    return jax.shard_map(
        per_device,
        mesh=mesh,
        in_specs=placed,
        out_specs=(
            P(("row", "col"), None),
            P("row", "col", None),
            P(("row", "col"), None),
            P(),
            P(),
            P(),
            P("col", None, None),
            P("col", None),
            P("col", None),
        ),
        check_vma=False,
    )
```

profile of v0, /device:TPU:8, one launch (start us, length us, event | category | flops | bytes accessed | tf_op | source)
XLA Modules:
  0.0 875.0 jit_solution(14454785513505962907)
XLA Ops:
  8.0 2.5 gather_fusion
  10.5 4.4 all-to-all-start
  15.7 5.4 all-to-all-done
  21.8 11.7 %all-to-all-start.1 = ((bf16[1,8,32,256]{3,1,0,2:T(8,128)(2,1)}), bf16[1,8,32,256]{3,1,0,2:T(8,128)(2,1)S(1)}, u32[]{:S(2)}, u32[]{:S(2)}) async-start(bf16[1,8,32,256]{3,1,0,2:T(8,128)(2,1)} %copy.26), calls=%async_computation.1 | async-start | bytes 262144 | tf_op jit(solution)/shard_map/all_to_all | solution.py:30
  34.7 7.9 all-to-all-done.1
  43.6 7.6 gather_fusion.1
  54.1 18.4 %all-gather.5.cloned.1.call-done = bf16[2048,256]{1,0:T(8,128)(2,1)} async-done(((bf16[256,256]{1,0:T(8,128)(2,1)}), bf16[2048,256]{1,0:T(8,128)(2,1)}) %all-gather.5.cloned.1.call-update) | async-done | bytes 1048592 | tf_op jit(solution)/shard_map/all_gather | solution.py:51
  72.6 32.2 %gather_fusion.3 = bf16[8192,256]{1,0:T(8,128)(2,1)} fusion(bf16[2048,256]{1,0:T(8,128)(2,1)} %all-gather.5.cloned.1.call-done, s32[8192]{0:T(1024)S(1)} %broadcast_clamp_fusion), kind=kCustom, calls=%fused_computation.3 | custom fusion | bytes 8421376 | tf_op jit(solution)/shard_map/gather | solution.py:52
  104.8 51.4 %all-gather.3.cloned.1.call-done = bf16[8192,256]{1,0:T(8,128)(2,1)} async-done(((bf16[256,256]{1,0:T(8,128)(2,1)}), bf16[8192,256]{1,0:T(8,128)(2,1)}) %all-gather.3.cloned.1.call-update) | async-done | bytes 4194320 | tf_op jit(solution)/shard_map/all_gather | solution.py:48
  156.2 33.6 %gather_fusion.2 = bf16[8192,256]{1,0:T(8,128)(2,1)} fusion(bf16[8192,256]{1,0:T(8,128)(2,1)} %all-gather.3.cloned.1.call-done, s32[8192]{0:T(1024)S(1)} %broadcast_clamp_fusion.1), kind=kCustom, calls=%fused_computation.2 | custom fusion | bytes 8421376 | tf_op jit(solution)/shard_map/gather | solution.py:50
  189.8 3.6 fusion.16
  194.7 2.4 fusion.6
  197.8 5.9 fusion.24
  205.6 4.5 fusion.1
  210.1 46.0 %scatter_custom_fusion.1 = f32[2048,256]{1,0:T(8,128)} fusion(s32[8192]{0:T(1024)S(1)} %bitcast.48, f32[8192,256]{1,0:T(8,128)} %fusion.1, f32[]{:T(128)} %constant.11.clone.1), kind=kCustom, calls=%fused_computation.25 | custom fusion | flops 2097152 | bytes 2097664 | tf_op jit(solution)/shard_map/scatter-add | solution.py:86
  256.4 6.7 fusion.2
  263.1 48.3 %scatter_custom_fusion = f32[8192,256]{1,0:T(8,128)} fusion(s32[8192]{0:T(1024)S(1)} %bitcast.46, f32[8192,256]{1,0:T(8,128)} %fusion.2, f32[]{:T(128)} %constant.11.clone.1), kind=kCustom, calls=%fused_computation.16 | custom fusion | flops 2097152 | bytes 8389120 | tf_op jit(solution)/shard_map/scatter-add | solution.py:80
  311.5 4.8 fusion.27
  316.3 221.9 %reduce-scatter.3.cloned.1.call-done = f32[256,256]{1,0:T(8,128)} async-done(((f32[8192,256]{1,0:T(8,128)}), f32[256,256]{1,0:T(8,128)}) %reduce-scatter.3.cloned.1.call-update) | async-done | bytes 262160 | tf_op jit(solution)/shard_map/reduce_scatter | solution.py:82
  541.3 4.8 fusion.28
  547.0 13.0 %all-reduce.1 = (f32[1,256]{1,0:T(1,128)}, f32[1,256]{1,0:T(1,128)}) all-reduce(f32[1,256]{1,0:T(1,128)S(1)} %bitcast.52, f32[1,256]{1,0:T(1,128)S(1)} %bitcast.53), channel_id=1, replica_groups=mesh['row'=8,'col'=32] {'row'}, use_global_device_ids=true, to_apply=%region_11.0 | all-reduce | flops 512 | bytes 4096 | tf_op jit(solution)/shard_map/psum | solution.py:70
  560.0 74.7 %psum.44 = f32[256]{0:T(256)} all-reduce(f32[256]{0:T(256)S(1)} %get-tuple-element.42), channel_id=1, replica_groups=mesh['row'=8,'col'=32] {'row','col'}, use_global_device_ids=true, to_apply=%region_8.0 | all-reduce | flops 256 | bytes 2048 | tf_op jit(solution)/shard_map/psum | solution.py:94
  634.6 162.6 %all-reduce.7.cloned.1.call-done = (f32[256,256]{0,1:T(8,128)}, f32[256,256]{1,0:T(8,128)}) async-done(((f32[256,256]{0,1:T(8,128)}, f32[256,256]{1,0:T(8,128)}), (f32[256,256]{0,1:T(8,128)}, f32[256,256]{1,0:T(8,128)})) %all-reduce.7.cloned.1.call-update) | async-done | bytes 524304 | tf_op jit(solution)/shard_map/psum | solution.py:94
  799.0 65.6 %all-reduce.5.cloned.1.call-done = f32[1,512,256]{2,1,0:T(8,128)} async-done(((f32[1,512,256]{2,1,0:T(8,128)}), f32[1,512,256]{2,1,0:T(8,128)}) %all-reduce.5.cloned.1.call-update) | async-done | bytes 524304 | tf_op jit(solution)/shard_map/psum | solution.py:70
  (70 shorter events, 19.9 us)
Async XLA Ops:
  7.2 26.4 %copy-start = (bf16[256,256]{1,0:T(8,128)(2,1)S(1)}, bf16[256,256]{1,0:T(8,128)(2,1)}, u32[]{:S(2)}) copy-start(bf16[256,256]{1,0:T(8,128)(2,1)} %param.17) | copy-start | bytes 393220
  7.2 44.2 %copy-start.13 = (f32[256]{0:T(256)S(1)}, f32[256]{0:T(256)}, u32[]{:S(2)}) copy-start(f32[256]{0:T(256)} %param.19) | copy-start | bytes 3076
  7.2 44.2 %copy-start.7 = (bf16[256,256]{1,0:T(8,128)(2,1)S(1)}, bf16[256,256]{1,0:T(8,128)(2,1)}, u32[]{:S(2)}) copy-start(bf16[256,256]{1,0:T(8,128)(2,1)} %param.18) | copy-start | bytes 393220
  10.5 42.7 %copy-start.14 = (bf16[256]{0:T(256)(128)(2,1)S(1)}, bf16[256]{0:T(256)(128)(2,1)}, u32[]{:S(2)}) copy-start(bf16[256]{0:T(256)(128)(2,1)} %param.22) | copy-start | bytes 1540
  10.5 43.4 %copy-start.10 = (s32[1,1,8192]{2,1,0:T(1,128)S(1)}, s32[1,1,8192]{2,1,0:T(1,128)}, u32[]{:S(2)}) copy-start(s32[1,1,8192]{2,1,0:T(1,128)} %param.27) | copy-start | bytes 98308
  10.5 43.4 %copy-start.8 = (s32[1,1,8192]{2,1,0:T(1,128)S(1)}, s32[1,1,8192]{2,1,0:T(1,128)}, u32[]{:S(2)}) copy-start(s32[1,1,8192]{2,1,0:T(1,128)} %param.25) | copy-start | bytes 98308
  10.5 43.5 %copy-start.9 = (s32[1,1,8192,1]{2,3,1,0:T(1,128)S(1)}, s32[1,1,8192,1]{2,3,1,0:T(1,128)}, u32[]{:S(2)}) copy-start(s32[1,1,8192,1]{2,3,1,0:T(1,128)} %param.24) | copy-start | bytes 98308
  10.5 43.5 %copy-start.11 = (s32[1,1,8192]{2,1,0:T(1,128)S(1)}, s32[1,1,8192]{2,1,0:T(1,128)}, u32[]{:S(2)}) copy-start(s32[1,1,8192]{2,1,0:T(1,128)} %param.26) | copy-start | bytes 98308
  10.5 10.6 %all-to-all-start = ((bf16[1,8,32,256]{3,2,0,1:T(8,128)(2,1)}), bf16[1,8,32,256]{3,2,0,1:T(8,128)(2,1)S(1)}, u32[]{:S(2)}, u32[]{:S(2)}) async-start(bf16[1,8,32,256]{3,2,0,1:T(8,128)(2,1)} %bitcast.3), calls=%async_computation | async-start | bytes 262144 | tf_op jit(solution)/shard_map/all_to_all | solution.py:31
  21.8 20.8 %all-to-all-start.1 = ((bf16[1,8,32,256]{3,1,0,2:T(8,128)(2,1)}), bf16[1,8,32,256]{3,1,0,2:T(8,128)(2,1)S(1)}, u32[]{:S(2)}, u32[]{:S(2)}) async-start(bf16[1,8,32,256]{3,1,0,2:T(8,128)(2,1)} %copy.26), calls=%async_computation.1 | async-start | bytes 262144 | tf_op jit(solution)/shard_map/all_to_all | solution.py:30
  33.6 39.0 %all-gather.5.cloned.1.call-start = ((), (), s32[]{:S(2)}) async-start(), calls=%async_computation.5 | async-start | bytes 1179648 | tf_op jit(solution)/shard_map/all_gather | solution.py:51
  52.3 103.9 %all-gather.3.cloned.1.call-start = ((), (), s32[]{:S(2)}) async-start(), calls=%async_computation.4 | async-start | bytes 4325376 | tf_op jit(solution)/shard_map/all_gather | solution.py:48
  53.0 263.3 %reduce-scatter.5.cloned.1.call-start = ((), (), s32[]{:S(2)}) async-start(), calls=%async_computation.7 | async-start | bytes 2359296 | tf_op jit(solution)/shard_map/reduce_scatter | solution.py:88
  104.8 85.0 %copy-start.6 = (bf16[512,256]{1,0:T(8,128)(2,1)S(1)}, bf16[512,256]{1,0:T(8,128)(2,1)}, u32[]{:S(2)}) copy-start(bf16[512,256]{1,0:T(8,128)(2,1)} %param.20) | copy-start | bytes 786436
  189.8 3.6 copy-start.3
  189.8 3.6 copy-start.12
  203.6 2.0 copy-start.2
  256.2 282.1 %reduce-scatter.3.cloned.1.call-start = ((), (), s32[]{:S(2)}) async-start(), calls=%async_computation.6 | async-start | bytes 8650752 | tf_op jit(solution)/shard_map/reduce_scatter | solution.py:82
  311.5 228.8 %copy-start.4 = (bf16[256,256]{1,0:T(8,128)(2,1)S(1)}, bf16[256,256]{1,0:T(8,128)(2,1)}, u32[]{:S(2)}) copy-start(bf16[256,256]{1,0:T(8,128)(2,1)} %param.14) | copy-start | bytes 393220
  311.5 485.7 %all-reduce.7.cloned.1.call-start = ((), (), s32[]{:S(2)}) async-start(), calls=%async_computation.9 | async-start | bytes 1048576 | tf_op jit(solution)/shard_map/psum | solution.py:94
  539.4 6.7 copy-start.5
  541.3 326.8 %copy-start.1 = (bf16[256,256]{1,0:T(8,128)(2,1)S(1)}, bf16[256,256]{1,0:T(8,128)(2,1)}, u32[]{:S(2)}) copy-start(bf16[256,256]{1,0:T(8,128)(2,1)} %param.17) | copy-start | bytes 393220
  541.3 323.3 %all-reduce.5.cloned.1.call-start = ((), (), s32[]{:S(2)}) async-start(), calls=%async_computation.8 | async-start | bytes 1048576 | tf_op jit(solution)/shard_map/psum | solution.py:70
Sparse Core Ops, SparseCore 0:
  52.4 20.1 all-gather.4
  75.7 80.4 all-gather.2
  256.3 34.6 reduce-scatter.4
  311.6 226.6 reduce-scatter.2
  545.3 251.9 all-reduce.6
  800.1 64.4 all-reduce.4
where the time goes:
time: 876 us; the launch traced here: 875 us
  waiting for transfers between devices  534 us (61%)
  other arithmetic  105 us (12%)
  blocking collectives  87.7 us (10%)
  local copies, waits for them, and re-layouts  84.1 us (10%)
  matrix products  31.8 us (4%)
  starting transfers between devices  16.8 us (2%)
  between operations  15.1 us (2%)
    reduce_scatter x1, waiting for transfers between devices, per_device(): src_grad = lax.psum_scatter(src_acc, 'col', scatter_dimension=0, tiled=True)  222 us
    psum x1, waiting for transfers between devices, per_device(): encoder_sums = lax.psum((part_self, part_neigh, part_bsage), ('row', 'col'))  163 us
    psum x1, blocking collectives, per_device(): encoder_sums = lax.psum((part_self, part_neigh, part_bsage), ('row', 'col'))  74.7 us
    psum x1, waiting for transfers between devices, per_device(): decoder_sums = lax.psum((part_first, part_bfirst, part_second), 'row')  65.6 us
    all_gather x1, waiting for transfers between devices, per_device(): src_block = lax.all_gather(embeds, 'col', axis=0, tiled=True)  51.4 us
    scatter-add x1, other arithmetic, per_device(): src_acc = jnp.zeros((src_block.shape[0], feat_width), jnp.float32).at[blo...  48.3 us
    scatter-add x1, other arithmetic, per_device(): dest_acc = jnp.zeros((dst_block.shape[0], feat_width), jnp.float32).at[de...  46 us
    gather x1, local copies, waits for them, and re-layouts, per_device(): src_embed = src_block[block_rows]  33.6 us
  transfers between devices with their start and end apart: 8, of which 7 were waited for; matrix products, arithmetic and copies ran while one was open for 12% of the time, Pallas kernels for 0%

commit v1 on v0

--- a/solution.py
+++ b/solution.py
@@ -48,7 +48,21 @@
     src_block = lax.all_gather(embeds, "col", axis=0, tiled=True)
     block_rows = owners * node_dev + local_rows
     src_embed = src_block[block_rows]
-    dst_block = lax.all_gather(embeds, "row", axis=0, tiled=True)
+    ways, here, step = (lax.axis_size("row"), lax.axis_index("row"), embeds.shape[0])
+    shape = [n * ways if d == 0 else n for d, n in enumerate(embeds.shape)]
+    full = lax.dynamic_update_slice_in_dim(
+        jnp.zeros(shape, embeds.dtype), embeds, here * step, axis=0
+    )
+    going_up = going_down = embeds
+    for far in range(1, ways // 2 + 1):
+        going_up = lax.ppermute(going_up, "row", [(d, (d + 1) % ways) for d in range(ways)])
+        full = lax.dynamic_update_slice_in_dim(full, going_up, (here - far) % ways * step, axis=0)
+        if 2 * far < ways:
+            going_down = lax.ppermute(going_down, "row", [(d, (d - 1) % ways) for d in range(ways)])
+            full = lax.dynamic_update_slice_in_dim(
+                full, going_down, (here + far) % ways * step, axis=0
+            )
+    dst_block = full
     dst_embed = dst_block[dest_rows]
     w_src = w_first[:feat_width]
     w_dst = w_first[feat_width:]

time: 876 us -> 846 us (0.966)
  waiting for transfers between devices: 534 us -> 498 us
    all_gather x1, waiting for transfers between devices: 51.4 us -> 18.1 us  [per_device(): src_block = lax.all_gather(embeds, 'col', axis=0, tiled=True)]
    all_gather x1 -> x0, waiting for transfers between devices: 18.4 us -> none  [per_device(): dst_block = lax.all_gather(embeds, 'row', axis=0, tiled=True)]
    ppermute x0 -> x7, waiting for transfers between devices: none -> 15.9 us  [the longest x4 11.1 us: per_device(): lax.ppermute(going_up, 'row', [(d, (d + 1) % ways) for d in range(ways)])]
  transfers between devices with their start and end apart: 8 -> 14, of which waited for: 7 -> 10; matrix products, arithmetic and copies ran while one was open for 12% -> 12% of each run, Pallas kernels for 0% -> 0%
where the time goes in v1:
time: 846 us
  waiting for transfers between devices  498 us (59%)
  other arithmetic  105 us (12%)
  blocking collectives  87.6 us (10%)
  local copies, waits for them, and re-layouts  84.9 us (10%)
  matrix products  31.9 us (4%)
  starting transfers between devices  23.3 us (3%)
  between operations  15 us (2%)
    reduce_scatter x1, waiting for transfers between devices, per_device(): src_grad = lax.psum_scatter(src_acc, 'col', scatter_dimension=0, tiled=True)  222 us
    psum x1, waiting for transfers between devices, per_device(): encoder_sums = lax.psum((part_self, part_neigh, part_bsage), ('row', 'col'))  163 us
    psum x1, blocking collectives, per_device(): encoder_sums = lax.psum((part_self, part_neigh, part_bsage), ('row', 'col'))  74.7 us
    psum x1, waiting for transfers between devices, per_device(): decoder_sums = lax.psum((part_first, part_bfirst, part_second), 'row')  65.6 us
    scatter-add x1, other arithmetic, per_device(): src_acc = jnp.zeros((src_block.shape[0], feat_width), jnp.float32).at[blo...  48.3 us
    scatter-add x1, other arithmetic, per_device(): dest_acc = jnp.zeros((dst_block.shape[0], feat_width), jnp.float32).at[de...  46 us
    gather x1, local copies, waits for them, and re-layouts, per_device(): src_embed = src_block[block_rows]  33.6 us
    gather x1, local copies, waits for them, and re-layouts, per_device(): dst_embed = dst_block[dest_rows]  32.9 us
  transfers between devices with their start and end apart: 14, of which 10 were waited for; matrix products, arithmetic and copies ran while one was open for 12% of the time, Pallas kernels for 0%

profile of v1, /device:TPU:8, one launch (start us, length us, event | category | flops | bytes accessed | tf_op | source)
XLA Modules:
  0.0 845.7 jit_solution(7698776016441500474)
XLA Ops:
  10.5 4.4 all-to-all-start
  15.6 5.4 all-to-all-done
  21.8 11.7 %all-to-all-start.1 = ((bf16[1,8,32,256]{3,1,0,2:T(8,128)(2,1)}), bf16[1,8,32,256]{3,1,0,2:T(8,128)(2,1)S(1)}, u32[]{:S(2)}, u32[]{:S(2)}) async-start(bf16[1,8,32,256]{3,1,0,2:T(8,128)(2,1)} %copy.26), calls=%async_computation.1 | async-start | bytes 262144 | tf_op jit(solution)/shard_map/all_to_all | solution.py:30
  34.8 7.8 all-to-all-done.1
  43.5 7.6 gather_fusion.1
  61.9 3.1 collective-permute-start.5
  65.0 5.6 collective-permute-done.4
  70.6 5.5 collective-permute-done.6
  76.2 32.9 %gather_fusion.3 = bf16[8192,256]{1,0:T(8,128)(2,1)} fusion(bf16[2048,256]{1,0:T(8,128)(2,1)S(1)} %constant_dynamic-update-slice_fusion, s32[8192]{0:T(1024)S(1)} %broadcast_clamp_fusion), kind=kCustom, calls=%fused_computation.3 | custom fusion | bytes 8421376 | tf_op jit(solution)/shard_map/gather | solution.py:66
  109.1 18.1 %all-gather.2.cloned.1.call-done = bf16[8192,256]{1,0:T(8,128)(2,1)} async-done(((bf16[256,256]{1,0:T(8,128)(2,1)}), bf16[8192,256]{1,0:T(8,128)(2,1)}) %all-gather.2.cloned.1.call-update) | async-done | bytes 4194320 | tf_op jit(solution)/shard_map/all_gather | solution.py:48
  127.2 33.6 %gather_fusion.2 = bf16[8192,256]{1,0:T(8,128)(2,1)} fusion(bf16[8192,256]{1,0:T(8,128)(2,1)} %all-gather.2.cloned.1.call-done, s32[8192]{0:T(1024)S(1)} %broadcast_clamp_fusion.1), kind=kCustom, calls=%fused_computation.2 | custom fusion | bytes 8421376 | tf_op jit(solution)/shard_map/gather | solution.py:50
  160.9 3.6 fusion.16
  168.8 5.9 fusion.24
  176.6 4.5 fusion.1
  181.2 46.0 %scatter_custom_fusion.1 = f32[2048,256]{1,0:T(8,128)} fusion(s32[8192]{0:T(1024)S(1)} %bitcast.48, f32[8192,256]{1,0:T(8,128)} %fusion.1, f32[]{:T(128)} %constant.68.clone.1), kind=kCustom, calls=%fused_computation.25 | custom fusion | flops 2097152 | bytes 2097664 | tf_op jit(solution)/shard_map/scatter-add | solution.py:100
  227.5 6.7 fusion.2
  234.2 48.3 %scatter_custom_fusion = f32[8192,256]{1,0:T(8,128)} fusion(s32[8192]{0:T(1024)S(1)} %bitcast.46, f32[8192,256]{1,0:T(8,128)} %fusion.2, f32[]{:T(128)} %constant.68.clone.1), kind=kCustom, calls=%fused_computation.16 | custom fusion | flops 2097152 | bytes 8389120 | tf_op jit(solution)/shard_map/scatter-add | solution.py:94
  282.6 4.8 fusion.27
  287.4 222.0 %reduce-scatter.3.cloned.1.call-done = f32[256,256]{1,0:T(8,128)} async-done(((f32[8192,256]{1,0:T(8,128)}), f32[256,256]{1,0:T(8,128)}) %reduce-scatter.3.cloned.1.call-update) | async-done | bytes 262160 | tf_op jit(solution)/shard_map/reduce_scatter | solution.py:96
  512.4 4.8 fusion.28
  518.1 13.0 %all-reduce.1 = (f32[1,256]{1,0:T(1,128)}, f32[1,256]{1,0:T(1,128)}) all-reduce(f32[1,256]{1,0:T(1,128)S(1)} %bitcast.52, f32[1,256]{1,0:T(1,128)S(1)} %bitcast.53), channel_id=1, replica_groups=mesh['row'=8,'col'=32] {'row'}, use_global_device_ids=true, to_apply=%region_11.12 | all-reduce | flops 512 | bytes 4096 | tf_op jit(solution)/shard_map/psum | solution.py:84
  531.1 74.7 %psum.44 = f32[256]{0:T(256)} all-reduce(f32[256]{0:T(256)S(1)} %get-tuple-element.42), channel_id=1, replica_groups=mesh['row'=8,'col'=32] {'row','col'}, use_global_device_ids=true, to_apply=%region_8.9 | all-reduce | flops 256 | bytes 2048 | tf_op jit(solution)/shard_map/psum | solution.py:108
  605.7 162.6 %all-reduce.7.cloned.1.call-done = (f32[256,256]{0,1:T(8,128)}, f32[256,256]{1,0:T(8,128)}) async-done(((f32[256,256]{0,1:T(8,128)}, f32[256,256]{1,0:T(8,128)}), (f32[256,256]{0,1:T(8,128)}, f32[256,256]{1,0:T(8,128)})) %all-reduce.7.cloned.1.call-update) | async-done | bytes 524304 | tf_op jit(solution)/shard_map/psum | solution.py:108
  770.1 65.6 %all-reduce.5.cloned.1.call-done = f32[1,512,256]{2,1,0:T(8,128)} async-done(((f32[1,512,256]{2,1,0:T(8,128)}), f32[1,512,256]{2,1,0:T(8,128)}) %all-reduce.5.cloned.1.call-update) | async-done | bytes 524304 | tf_op jit(solution)/shard_map/psum | solution.py:84
  (87 shorter events, 32.7 us)
Async XLA Ops:
  7.2 44.2 %copy-start = (bf16[256,256]{1,0:T(8,128)(2,1)S(1)}, bf16[256,256]{1,0:T(8,128)(2,1)}, u32[]{:S(2)}) copy-start(bf16[256,256]{1,0:T(8,128)(2,1)} %param.18) | copy-start | bytes 393220
  10.5 40.9 %copy-start.12 = (f32[256]{0:T(256)S(1)}, f32[256]{0:T(256)}, u32[]{:S(2)}) copy-start(f32[256]{0:T(256)} %param.19) | copy-start | bytes 3076
  10.5 10.6 %all-to-all-start = ((bf16[1,8,32,256]{3,2,0,1:T(8,128)(2,1)}), bf16[1,8,32,256]{3,2,0,1:T(8,128)(2,1)S(1)}, u32[]{:S(2)}, u32[]{:S(2)}) async-start(bf16[1,8,32,256]{3,2,0,1:T(8,128)(2,1)} %bitcast.3), calls=%async_computation | async-start | bytes 262144 | tf_op jit(solution)/shard_map/all_to_all | solution.py:31
  21.8 20.8 %all-to-all-start.1 = ((bf16[1,8,32,256]{3,1,0,2:T(8,128)(2,1)}), bf16[1,8,32,256]{3,1,0,2:T(8,128)(2,1)S(1)}, u32[]{:S(2)}, u32[]{:S(2)}) async-start(bf16[1,8,32,256]{3,1,0,2:T(8,128)(2,1)} %copy.26), calls=%async_computation.1 | async-start | bytes 262144 | tf_op jit(solution)/shard_map/all_to_all | solution.py:30
  33.5 93.7 %all-gather.2.cloned.1.call-start = ((), (), s32[]{:S(2)}) async-start(), calls=%async_computation.4 | async-start | bytes 4325376 | tf_op jit(solution)/shard_map/all_gather | solution.py:48
  33.5 19.1 %copy-start.13 = (bf16[256]{0:T(256)(128)(2,1)S(1)}, bf16[256]{0:T(256)(128)(2,1)}, u32[]{:S(2)}) copy-start(bf16[256]{0:T(256)(128)(2,1)} %param.22) | copy-start | bytes 1540
  33.6 19.7 %copy-start.9 = (s32[1,1,8192]{2,1,0:T(1,128)S(1)}, s32[1,1,8192]{2,1,0:T(1,128)}, u32[]{:S(2)}) copy-start(s32[1,1,8192]{2,1,0:T(1,128)} %param.27) | copy-start | bytes 98308
  34.7 18.6 %copy-start.7 = (s32[1,1,8192]{2,1,0:T(1,128)S(1)}, s32[1,1,8192]{2,1,0:T(1,128)}, u32[]{:S(2)}) copy-start(s32[1,1,8192]{2,1,0:T(1,128)} %param.25) | copy-start | bytes 98308
  34.7 18.6 %copy-start.8 = (s32[1,1,8192,1]{2,3,1,0:T(1,128)S(1)}, s32[1,1,8192,1]{2,3,1,0:T(1,128)}, u32[]{:S(2)}) copy-start(s32[1,1,8192,1]{2,3,1,0:T(1,128)} %param.24) | copy-start | bytes 98308
  34.8 18.7 %copy-start.10 = (s32[1,1,8192]{2,1,0:T(1,128)S(1)}, s32[1,1,8192]{2,1,0:T(1,128)}, u32[]{:S(2)}) copy-start(s32[1,1,8192]{2,1,0:T(1,128)} %param.26) | copy-start | bytes 98308
  52.3 235.1 %reduce-scatter.5.cloned.1.call-start = ((), (), s32[]{:S(2)}) async-start(), calls=%async_computation.6 | async-start | bytes 2359296 | tf_op jit(solution)/shard_map/reduce_scatter | solution.py:102
  53.5 2.9 collective-permute-start.1
  53.6 5.8 collective-permute-start
  56.4 5.5 collective-permute-start.3
  59.4 5.6 collective-permute-start.2
  61.9 8.7 %collective-permute-start.5 = (bf16[256,256]{1,0:T(8,128)(2,1)S(1)}, bf16[256,256]{1,0:T(8,128)(2,1)S(1)}, u32[]{:S(2)}, u32[]{:S(2)}) collective-permute-start(bf16[256,256]{1,0:T(8,128)(2,1)S(1)} %collective-permute-done.3), channel_id=1, source_target_pairs={{0,224},{32,0},{64,32},{96,64},{128,96},{160,128},{192,160},{224,1... | collective-permute-start | bytes 393224 | tf_op jit(solution)/shard_map/ppermute | solution.py:61
  65.0 5.6 collective-permute-start.4
  70.6 5.6 collective-permute-start.6
  109.1 51.8 %copy-start.6 = (bf16[512,256]{1,0:T(8,128)(2,1)S(1)}, bf16[512,256]{1,0:T(8,128)(2,1)}, u32[]{:S(2)}) copy-start(bf16[512,256]{1,0:T(8,128)(2,1)} %param.20) | copy-start | bytes 786436
  227.2 282.2 %reduce-scatter.3.cloned.1.call-start = ((), (), s32[]{:S(2)}) async-start(), calls=%async_computation.5 | async-start | bytes 8650752 | tf_op jit(solution)/shard_map/reduce_scatter | solution.py:96
  282.5 228.9 %copy-start.4 = (bf16[256,256]{1,0:T(8,128)(2,1)S(1)}, bf16[256,256]{1,0:T(8,128)(2,1)}, u32[]{:S(2)}) copy-start(bf16[256,256]{1,0:T(8,128)(2,1)} %param.14) | copy-start | bytes 393220
  282.5 485.8 %all-reduce.7.cloned.1.call-start = ((), (), s32[]{:S(2)}) async-start(), calls=%async_computation.8 | async-start | bytes 1048576 | tf_op jit(solution)/shard_map/psum | solution.py:108
  512.4 326.8 %copy-start.1 = (bf16[256,256]{1,0:T(8,128)(2,1)S(1)}, bf16[256,256]{1,0:T(8,128)(2,1)}, u32[]{:S(2)}) copy-start(bf16[256,256]{1,0:T(8,128)(2,1)} %param.18) | copy-start | bytes 393220
  512.4 323.3 %all-reduce.5.cloned.1.call-start = ((), (), s32[]{:S(2)}) async-start(), calls=%async_computation.7 | async-start | bytes 1048576 | tf_op jit(solution)/shard_map/psum | solution.py:84
  (4 other events, 15.9 us)
Sparse Core Ops, SparseCore 0:
  52.4 74.7 all-gather.1
  227.3 34.6 reduce-scatter.4
  282.6 226.7 reduce-scatter.2
  516.4 251.8 all-reduce.6
  771.2 64.4 all-reduce.4
